TPU v7x, 32 devices: a whole 2x2x4 slice. The times are simulated.
32 devices in a mesh: fsdp: 16 (over z, y, core), grp: 2 (over x).
Axes of the slice: x: 2, y: 2, z: 4, core: 2. Of those that a mesh axis runs over, the one named last changes fastest.
Arguments:
- hidden_act: bfloat16 [2, 2048, 14336], P('grp', None, 'fsdp'), may hold values from -6 to 6
- grad_output: bfloat16 [2, 2048, 4096], P('grp', 'fsdp'), may hold values from -6 to 6
- down_weight: bfloat16 [14336, 4096], P('fsdp'), may hold values from -0.09375 to 0.09375
- proj_in: bfloat16 [14336, 64], P('fsdp'), may hold values from -0.046875 to 0.046875
- proj_out: bfloat16 [4096, 64], replicated, may hold values from -0.09375 to 0.09375
- example_ids: int32 [2, 2048], P('grp'), may hold values from 0 to 7, never falling along the last dimension, each value on 1 to 512 neighbouring positions
Outputs:
- grad_hidden: bfloat16 [2, 2048, 14336], P('grp', None, 'fsdp')
- gram: float32 [4096, 4096], P('grp', 'fsdp')
- scores: float32 [16], replicated
Inputs may be any that keep to these rules, and one draw needn't show every extreme that they name: `example_ids`: never falls along a group's tokens; each of the 8 examples of a group has 1 to 512 tokens, one exactly 512.
All inputs are finite; a program needn't handle non-finite values.
Results may differ from a plain program's by a relative error of at most 0.001.
Values may be sent and summed in bfloat16 or wider, within the bound.
A program may use at most 128 MiB of HBM per device.

v0:
```python
import jax
import jax.numpy as jnp
from jax import lax
from jax.sharding import PartitionSpec as P

PROJ = 64
TOK_GRP = 2048
EX_GRP = 8


def inverse_diagonal(matrix):
    lower = jnp.linalg.cholesky(matrix)
    eye = jnp.eye(matrix.shape[0], dtype=matrix.dtype)
    lower_inv = jax.scipy.linalg.solve_triangular(lower, eye, lower=True)
    return jnp.sum(lower_inv * lower_inv, axis=0)


def example_features(ids, left, right):
    onehot = (jnp.arange(EX_GRP, dtype=jnp.int32)[:, None] == ids[None, :]).astype(jnp.float32)
    weighted = (onehot[:, None, :] * jnp.transpose(left)[None, :, :]).reshape(
        EX_GRP * PROJ, ids.shape[0]
    )
    product = jnp.dot(weighted, right, precision=lax.Precision.HIGHEST)
    return product.reshape(EX_GRP, PROJ * PROJ) * (EX_GRP / TOK_GRP) ** 0.5


def body(hidden_act, grad_output, down_weight, proj_in, proj_out, example_ids):
    fsdp_count = lax.axis_size("fsdp")
    group_count = lax.axis_size("grp")
    hidden_rows = hidden_act[0]
    grad_rows = grad_output[0]
    group_ids = example_ids[0]
    tok_rows = grad_rows.shape[0]
    feat_width = PROJ * PROJ
    examples = EX_GRP * group_count
    grad_full = lax.all_gather(grad_rows, "fsdp", axis=0, tiled=True)
    grad_hidden = lax.dot_general(
        grad_full, down_weight, (((1,), (1,)), ((), ())), preferred_element_type=jnp.float32
    )
    grad_hidden = grad_hidden.astype(jnp.bfloat16)[None]
    rows_part = hidden_rows
    left = lax.psum_scatter(
        jnp.dot(rows_part, proj_in, preferred_element_type=jnp.float32),
        "fsdp",
        scatter_dimension=0,
        tiled=True,
    )
    right = jnp.dot(grad_rows, proj_out, preferred_element_type=jnp.float32)
    my_ids = lax.dynamic_slice_in_dim(group_ids, lax.axis_index("fsdp") * tok_rows, tok_rows, 0)
    partial_feats = example_features(my_ids, left, right)
    col_count = feat_width // fsdp_count
    group_feats = lax.psum(partial_feats, "fsdp")
    all_feats = lax.all_gather(group_feats.astype(jnp.bfloat16), "grp", axis=0, tiled=True).astype(
        group_feats.dtype
    )
    own_cols = lax.dynamic_slice_in_dim(
        group_feats, lax.axis_index("fsdp") * col_count, col_count, 1
    )
    rows_part = group_feats
    product = lax.dot_general(
        rows_part,
        own_cols,
        (((0,), (0,)), ((), ())),
        precision=lax.Precision.HIGHEST,
        preferred_element_type=jnp.float32,
    )
    gram = lax.psum_scatter(product / examples, "grp", scatter_dimension=0, tiled=True)
    kernel = lax.dot_general(
        all_feats,
        all_feats,
        (((1,), (1,)), ((), ())),
        precision=lax.Precision.HIGHEST,
        preferred_element_type=jnp.float32,
    )
    ridge = jnp.trace(kernel) / examples
    eye = jnp.eye(examples, dtype=jnp.float32)
    scores = 1.0 - ridge * inverse_diagonal(kernel + ridge * eye)
    return (grad_hidden, gram, scores)


def solution(mesh):
    in_specs = (
        P("grp", None, "fsdp"),
        P("grp", "fsdp", None),
        P("fsdp", None),
        P("fsdp", None),
        P(),
        P("grp", None),
    )
    out_specs = (P("grp", None, "fsdp"), P("grp", "fsdp"), P())
    return jax.shard_map(body, mesh=mesh, in_specs=in_specs, out_specs=out_specs, check_vma=False)
```

profile of v0, /device:TPU:0, one launch (start us, length us, event | category | flops | bytes accessed | tf_op | source)
XLA Modules:
  0.0 354.3 jit_solution(14325291054857853550)
XLA Ops:
  7.2 0.0 copy-start
  7.2 0.0 copy-start.1
  7.2 0.0 reduce-scatter.3.cloned.1.call-start
  7.2 4.2 %fusion.2 = f32[2048,64]{0,1:T(8,128)} fusion(bf16[896,64]{0,1:T(8,128)(2,1)} %param.9, bf16[1,2048,896]{2,1,0:T(8,128)(2,1)} %param.6), kind=kOutput, calls=%fused_computation.3 | convolution fusion | flops 234881024 | bytes 4308992 | tf_op jit(solution)/shard_map/dot_general | solution.py:43
  11.4 0.0 reduce-scatter.3.cloned.1.call-update
  11.4 0.0 all-reduce.2.cloned.1.call-start
  11.5 0.7 dynamic-slice_bitcast_fusion
  12.2 0.0 copy-done
  12.2 0.0 copy-done.1
  12.2 0.4 fusion.7
  12.6 58.1 %reduce-scatter.3.cloned.1.call-done = f32[128,64]{0,1:T(8,128)} async-done(((f32[2048,64]{0,1:T(8,128)}), f32[128,64]{0,1:T(8,128)}) %reduce-scatter.3.cloned.1.call-update) | async-done | bytes 32784 | tf_op jit(solution)/shard_map/reduce_scatter | solution.py:42
  70.7 0.8 broadcast_multiply_fusion
  71.5 0.4 convolution_multiply_fusion.1
  71.9 0.1 copy.10
  72.0 0.8 mul.56
  72.8 0.0 all-reduce.2.cloned.1.call-update
  72.8 0.0 all-gather.3.cloned.1.call-start
  72.9 0.7 all-gather.3.cloned.1.call-update
  73.6 0.0 reduce-scatter.5.cloned.1.call-start
  73.6 87.4 %all-reduce.2.cloned.1.call-done = f32[8,4096]{1,0:T(8,128)} async-done(((f32[8,4096]{1,0:T(8,128)}), f32[8,4096]{1,0:T(8,128)}) %all-reduce.2.cloned.1.call-update) | async-done | bytes 131088 | tf_op jit(solution)/shard_map/psum | solution.py:52
  161.0 0.0 copy-start.2
  161.0 6.4 %convolution_multiply_fusion = f32[4096,256]{1,0:T(8,128)} fusion(f32[8,4096]{1,0:T(8,128)} %all-reduce.2.cloned.1.call-done, s32[]{:T(128)S(6)} %select_n.16), kind=kOutput, calls=%fused_computation.2 | convolution fusion | flops 101711872 | bytes 4333572 | tf_op jit(solution)/shard_map/dot_general | solution.py:60
  167.4 0.0 reduce-scatter.5.cloned.1.call-update
  167.4 0.0 copy-done.2
  167.5 5.0 %all_gather.7 = bf16[16,4096]{1,0:T(8,128)(2,1)S(1)} all-gather(bf16[8,4096]{1,0:T(8,128)(2,1)S(1)} %convert_element_type.18), channel_id=1, replica_groups=mesh['fsdp'=16,'grp'=2] {'grp'}, dimensions={0}, use_global_device_ids=true | all-gather | bytes 196608 | tf_op jit(solution)/shard_map/all_gather | solution.py:53
  172.5 0.8 select_reduce_fusion.1
  173.2 0.1 copy.11
  174.0 1.4 cholesky.13
  175.5 0.6 compare_reduce_fusion
  176.1 0.6 fusion.9
  176.8 1.2 custom-call.7
  178.0 0.2 fusion.6
  178.2 0.5 multiply_subtract_fusion
  178.7 113.7 %all-gather.3.cloned.1.call-done = bf16[1,2048,4096]{2,1,0:T(8,128)(2,1)} async-done(((bf16[1,128,4096]{2,1,0:T(8,128)(2,1)}), bf16[1,2048,4096]{2,1,0:T(8,128)(2,1)}) %all-gather.3.cloned.1.call-update) | async-done | bytes 16777232 | tf_op jit(solution)/shard_map/all_gather | solution.py:36
  292.4 23.4 %convert_bitcast_fusion = bf16[1,2048,896]{2,1,0:T(8,128)(2,1)} fusion(bf16[896,4096]{1,0:T(8,128)(2,1)} %param.8, bf16[1,2048,4096]{2,1,0:T(8,128)(2,1)} %all-gather.3.cloned.1.call-done), kind=kOutput, calls=%fused_computation.5 | convolution fusion | flops 15034220544 | bytes 27787264 | tf_op jit(solution)/shard_map/dot_general | solution.py:37
  315.8 31.9 %reduce-scatter.5.cloned.1.call-done = f32[2048,256]{1,0:T(8,128)} async-done(((f32[4096,256]{1,0:T(8,128)}), f32[2048,256]{1,0:T(8,128)}) %reduce-scatter.5.cloned.1.call-update) | async-done | bytes 2097168 | tf_op jit(solution)/shard_map/reduce_scatter | solution.py:67
  (4 shorter events, 0.1 us)
Async XLA Ops:
  7.2 5.0 %copy-start = (bf16[4096,64]{0,1:T(8,128)(2,1)S(1)}, bf16[4096,64]{0,1:T(8,128)(2,1)}, u32[]{:S(2)}) copy-start(bf16[4096,64]{0,1:T(8,128)(2,1)} %param.10) | copy-start | bytes 1572868
  7.2 5.0 %copy-start.1 = (bf16[1,128,4096]{2,1,0:T(8,128)(2,1)S(1)}, bf16[1,128,4096]{2,1,0:T(8,128)(2,1)}, u32[]{:S(2)}) copy-start(bf16[1,128,4096]{2,1,0:T(8,128)(2,1)} %param.7) | copy-start | bytes 3145732
  7.2 63.5 %reduce-scatter.3.cloned.1.call-start = ((), (), s32[]{:S(2)}) async-start(), calls=%async_computation.2 | async-start | bytes 557056 | tf_op jit(solution)/shard_map/reduce_scatter | solution.py:42
  11.4 149.6 %all-reduce.2.cloned.1.call-start = ((), (), s32[]{:S(2)}) async-start(), calls=%async_computation.3 | async-start | bytes 262144 | tf_op jit(solution)/shard_map/psum | solution.py:52
  72.8 219.6 %all-gather.3.cloned.1.call-start = ((), (), s32[]{:S(2)}) async-start(), calls=%async_computation.5 | async-start | bytes 17825792 | tf_op jit(solution)/shard_map/all_gather | solution.py:36
  73.6 274.2 %reduce-scatter.5.cloned.1.call-start = ((), (), s32[]{:S(2)}) async-start(), calls=%async_computation.4 | async-start | bytes 6291456 | tf_op jit(solution)/shard_map/reduce_scatter | solution.py:67
  161.0 6.4 %copy-start.2 = (f32[8,4096]{1,0:T(8,128)S(1)}, f32[8,4096]{1,0:T(8,128)}, u32[]{:S(2)}) copy-start(f32[8,4096]{1,0:T(8,128)} %all-reduce.2.cloned.1.call-done) | copy-start | bytes 393220
Sparse Core Ops, SparseCore 0:
  12.1 58.4 reduce-scatter.2
  75.1 85.8 all-reduce.1
  163.4 128.9 all-gather.2
  295.2 52.4 reduce-scatter.4
where the time goes:
time: 354 us
  waiting for transfers between devices  292 us (82%)
  matrix products  35.8 us (10%)
  between operations  14.5 us (4%)
  other arithmetic  5.33 us (2%)
  blocking collectives  5 us (1%)
    all_gather x1, waiting for transfers between devices, body(): grad_full = lax.all_gather(grad_rows, 'fsdp', axis=0, tiled=True)  114 us
    psum x1, waiting for transfers between devices, body(): group_feats = lax.psum(partial_feats, 'fsdp')  87.4 us
    reduce_scatter x1, waiting for transfers between devices, body(): lax.psum_scatter(jnp.dot(rows_part, proj_in, preferred_element_type=jnp.f...  58.1 us
    reduce_scatter x1, waiting for transfers between devices, body(): lax.psum_scatter(product / examples, 'grp', scatter_dimension=0, tiled=True)  31.9 us
    dot_general x1, matrix products, body(): lax.dot_general(grad_full, down_weight, (((1,), (1,)), ((), ())), preferr...  23.4 us
  transfers between devices with their start and end apart: 4, of which 4 were waited for; matrix products, arithmetic and copies ran while one was open for 10% of the time, Pallas kernels for 0%

commit v1 on v0

v1 whole, which is shorter than its diff:
```python
import functools

import jax
import jax.numpy as jnp
from jax import lax
from jax.experimental import pallas as pl
from jax.experimental.pallas import tpu as pltpu
from jax.sharding import PartitionSpec as P

PROJ = 64
EX_GRP = 8
LANES = 128
MESH = pl.DeviceIdType.MESH
HIGH = lax.Precision.HIGHEST
NT = (((1,), (1,)), ((), ()))
TN = (((0,), (0,)), ((), ()))


def dot(a, b, dims, precision=None):
    return lax.dot_general(a, b, dims, precision=precision, preferred_element_type=jnp.float32)


def kernel(
    n, groups, scale,
    x_hbm, w_hbm, h_hbm, pin_hbm, pout_hbm, ids_ref,
    out_ref, gram_ref, score_ref,
    gath, own, w, h, pin, pout, rts, part, red, cross, feats, flat,
    local_sem, ring_send, ring_recv, sib_send, sib_recv, own_send, own_recv,
    rt_send, rt_recv, red_send, red_recv, x_send, x_recv, f_send, f_recv,
):
    chips = n // 2
    steps = chips - 1
    half_chips = chips // 2
    rows = x_hbm.shape[0]
    half = rows // 2
    width = w_hbm.shape[0]
    chunks = part.shape[0] // n
    examples = groups * EX_GRP
    gram_rows = gram_ref.shape[0]

    me = lax.axis_index("fsdp")
    grp = lax.axis_index("grp")
    core = lax.rem(me, 2)
    chip = lax.div(me, 2)
    side = lax.rem(chip, 2)
    along = lax.div(chip, 2)
    pos = (1 - side) * along + side * (chips - 1 - along)

    def chip_at(p):
        p = lax.rem(p + chips, chips)
        back = lax.div(p, half_chips)
        return (1 - back) * (2 * p) + back * (2 * (chips - 1 - p) + 1)

    right = chip_at(pos + 1) * 2 + core
    left = chip_at(pos - 1) * 2 + core
    sibling = chip * 2 + (1 - core)

    def peer(p):
        return lax.rem(me + p, n)

    def source(p):
        return lax.rem(me + n - p, n)

    def remote(src, dst, send, recv, **where):
        return pltpu.make_async_remote_copy(
            src_ref=src, dst_ref=dst, send_sem=send, recv_sem=recv,
            device_id=where, device_id_type=MESH,
        )

    loads = [
        pltpu.make_async_copy(src, dst, local_sem.at[i])
        for i, (src, dst) in enumerate(
            ((x_hbm, own.at[0]), (pout_hbm, pout), (h_hbm, h), (pin_hbm, pin), (w_hbm, w))
        )
    ]
    for load in loads:
        load.start()

    barrier = pltpu.get_barrier_semaphore()

    def greet(p, carry):
        pl.semaphore_signal(barrier, inc=1, device_id={"fsdp": peer(p)}, device_id_type=MESH)
        return carry

    lax.fori_loop(1, n, greet, 0)
    for k in range(1, groups):
        pl.semaphore_signal(
            barrier, inc=1, device_id={"grp": lax.rem(grp + k, groups)}, device_id_type=MESH
        )
    pl.semaphore_wait(barrier, n - 1 + groups - 1)

    def first(s, way):
        part_of = s % 2 if way == 0 else 1 - s % 2
        return remote(
            x_hbm.at[pl.ds(part_of * half, half)], gath.at[s, way, 0],
            ring_send.at[s, way], ring_recv.at[s, way], fsdp=right if way == 0 else left,
        )

    def onward(s, way):
        return remote(
            gath.at[s - 2, way, 0], gath.at[s, way, 0],
            ring_send.at[s, way], ring_recv.at[s, way], fsdp=right if way == 0 else left,
        )

    def across(s, way):
        return remote(
            gath.at[s, way, 0], gath.at[s, way, 1],
            sib_send.at[s, way], sib_recv.at[s, way], fsdp=sibling,
        )

    for s in range(min(2, steps)):
        for way in range(2):
            first(s, way).start()
    own_copy = remote(x_hbm, own.at[1], own_send, own_recv, fsdp=sibling)
    own_copy.start()

    def rt_copy(p):
        return remote(rts.at[me], rts.at[me], rt_send.at[p - 1], rt_recv.at[p - 1], fsdp=peer(p))

    def red_copy(p):
        return remote(
            part.at[pl.ds(peer(p) * chunks, chunks)], red.at[me],
            red_send.at[p - 1], red_recv.at[p - 1], fsdp=peer(p),
        )

    def x_copy(k):
        return remote(
            cross.at[grp], cross.at[grp], x_send.at[k - 1], x_recv.at[k - 1],
            grp=lax.rem(grp + k, groups),
        )

    def f_copy(p):
        return remote(
            feats.at[me], feats.at[me], f_send.at[p - 1], f_recv.at[p - 1], fsdp=peer(p)
        )

    def over_peers(action):
        def step(p, carry):
            action(p)
            return carry

        lax.fori_loop(1, n, step, 0)

    loads[0].wait()
    loads[1].wait()
    rts[me] = dot(pout[...], own[0], NT)
    over_peers(lambda p: rt_copy(p).start())

    def multiply(block, places):
        count = len(places)
        size = block.shape[0] // count
        for start in range(0, width, 256):
            stop = min(width, start + 256)
            product = dot(block, w[start:stop, :], NT).astype(out_ref.dtype)
            for i, place in enumerate(places):
                out_ref[pl.ds(pl.multiple_of(place, size), size), start:stop] = product[
                    i * size:(i + 1) * size
                ]

    loads[4].wait()
    own_copy.wait_recv()
    multiply(own[...].reshape(2 * rows, -1), (me * rows, sibling * rows))

    def partial_feats():
        loads[2].wait()
        loads[3].wait()
        over_peers(lambda p: rt_copy(p).wait_recv())
        r = lax.broadcasted_iota(jnp.int32, (PROJ, PROJ), 0)
        c = lax.broadcasted_iota(jnp.int32, (PROJ, PROJ), 1)
        mid = PROJ // 2
        wanted = jnp.where(r < mid, 2 * r, 2 * (r - mid) + 1)
        order = jnp.where(c == wanted, 1.0, 0.0).astype(jnp.bfloat16)
        sorted_in = lax.dot_general(
            order, pin[...], (((1,), (0,)), ((), ())), preferred_element_type=jnp.float32
        ).astype(jnp.bfloat16)
        part[...] = jnp.zeros_like(part)
        which = lax.broadcasted_iota(jnp.int32, (EX_GRP, rows), 0)
        blank = jnp.zeros((PROJ, rows), jnp.float32)

        def block(b, carry):
            piece = h[pl.ds(pl.multiple_of(b * rows, rows), rows), :]
            left_t = dot(sorted_in, piece, NT)
            onehot = jnp.where(ids_ref[b] == which, 1.0, 0.0)
            right_t = rts[b]
            total = part[...].reshape(mid * EX_GRP, LANES)
            for i, pair in enumerate(((right_t, blank), (blank, right_t))):
                rows_of = left_t[i * mid:(i + 1) * mid]
                weighted = (rows_of[:, None, :] * onehot[None]).reshape(mid * EX_GRP, rows)
                total += dot(weighted, jnp.concatenate(pair, axis=0), NT, HIGH)
            part[...] = total.reshape(part.shape)
            return carry

        lax.fori_loop(0, n, block, 0)
        over_peers(lambda p: red_copy(p).start())

    def reduce_feats():
        over_peers(lambda p: red_copy(p).wait_recv())
        total = part[pl.ds(me * chunks, chunks)]

        def add(p, total):
            return total + red[source(p)]

        cross[grp] = lax.fori_loop(1, n, add, total) * scale
        for k in range(1, groups):
            x_copy(k).start()

    def share_feats():
        for k in range(1, groups):
            x_copy(k).wait_recv()
        feats[me] = cross[...]
        over_peers(lambda p: f_copy(p).start())

    def gram_block():
        over_peers(lambda p: f_copy(p).wait_recv())
        for q in range(n):
            for m in range(chunks):
                column = (q * chunks + m) * LANES
                flat[:, column:column + LANES] = feats[q, :, m].reshape(examples, LANES)
        cols = chunks * LANES
        mine = flat[:, pl.ds(pl.multiple_of(me * cols, cols), cols)] * (1.0 / examples)
        tile = min(512, gram_rows)

        def rows_of(t, carry):
            at = pl.multiple_of(grp * gram_rows + t * tile, tile)
            gram_ref[pl.ds(pl.multiple_of(t * tile, tile), tile), :] = dot(
                flat[:, pl.ds(at, tile)], mine, TN, HIGH
            )
            return carry

        lax.fori_loop(0, gram_rows // tile, rows_of, 0)

    def score():
        every = flat[...]
        matrix = dot(every, every, NT, HIGH)
        r = lax.broadcasted_iota(jnp.int32, (examples, examples), 0)
        c = lax.broadcasted_iota(jnp.int32, (examples, examples), 1)
        diagonal = jnp.where(r == c, matrix, 0.0)
        ridge = jnp.sum(jnp.sum(diagonal, axis=1, keepdims=True), axis=0, keepdims=True)
        ridge = ridge * (1.0 / examples)
        matrix = matrix + jnp.where(r == c, ridge, 0.0)
        c1 = lax.broadcasted_iota(jnp.int32, (1, examples), 1)

        def eliminate(j, a):
            row = jnp.sum(jnp.where(r == j, a, 0.0), axis=0, keepdims=True)
            col = jnp.sum(jnp.where(c == j, a, 0.0), axis=1, keepdims=True)
            pivot = jnp.sum(jnp.where(c1 == j, row, 0.0), axis=1, keepdims=True)
            row = jnp.where(c1 == j, 1.0, row) / pivot
            return jnp.where(r == j, row, jnp.where(c == j, 0.0, a) - col * row)

        inverse = lax.fori_loop(0, examples, eliminate, matrix)
        diagonal = jnp.sum(jnp.where(r == c, inverse, 0.0), axis=0, keepdims=True)
        score_ref[...] = 1.0 - ridge * diagonal

    phases = (partial_feats, reduce_feats, share_feats, gram_block, score)

    def places(s):
        distance = lax.div(s, 2) + 1
        which = lax.rem(s, 2)
        found = []
        for way in range(2):
            at = chip_at(pos - distance if way == 0 else pos + distance)
            offset = (which if way == 0 else 1 - which) * half
            found.append((at * 2 + core) * rows + offset)
            found.append((at * 2 + 1 - core) * rows + offset)
        return found

    def finish(s):
        for way in range(2):
            across(s, way).wait_recv()
        multiply(gath[s].reshape(4 * half, -1), places(s))

    def ring(s, carry):
        for way in range(2):
            remote(
                gath.at[s, way, 0], gath.at[s, way, 0],
                ring_send.at[s, way], ring_recv.at[s, way], fsdp=right if way == 0 else left,
            ).wait_recv()

            @pl.when(s + 2 < steps)
            def _():
                onward(s + 2, way).start()

            across(s, way).start()

        for k, phase in enumerate(phases):
            pl.when(s == min(k, steps - 1))(phase)

        @pl.when(s > 0)
        def _():
            finish(s - 1)

        return carry

    lax.fori_loop(0, steps, ring, 0)
    finish(steps - 1)

    def sent(s, carry):
        for way in range(2):
            across(s, way).wait_send()

        return carry

    lax.fori_loop(0, steps, sent, 0)
    for s in range(min(2, steps)):
        for way in range(2):
            first(s, way).wait_send()

    def sent_on(s, carry):
        for way in range(2):
            onward(s, way).wait_send()
        return carry

    lax.fori_loop(2, steps, sent_on, 0)
    own_copy.wait_send()
    for copies in (rt_copy, red_copy, f_copy):
        over_peers(lambda p: copies(p).wait_send())
    for k in range(1, groups):
        x_copy(k).wait_send()


def body(hidden_act, grad_output, down_weight, proj_in, proj_out, example_ids):
    n = lax.axis_size("fsdp")
    groups = lax.axis_size("grp")
    h = hidden_act[0]
    x = grad_output[0]
    rows, depth = x.shape
    tokens, width = h.shape
    steps = n // 2 - 1
    feat_width = PROJ * PROJ
    examples = EX_GRP * groups
    chunks = feat_width // LANES // n
    scale = (EX_GRP / tokens) ** 0.5
    ids = example_ids.reshape(n, 1, rows)
    f32, bf16 = jnp.float32, jnp.bfloat16
    dma = pltpu.SemaphoreType.DMA
    vmem = pl.BlockSpec(memory_space=pltpu.VMEM)
    hbm = pl.BlockSpec(memory_space=pl.ANY)
    out, gram, scores = pl.pallas_call(
        functools.partial(kernel, n, groups, scale),
        out_shape=(
            jax.ShapeDtypeStruct((tokens, width), bf16),
            jax.ShapeDtypeStruct((feat_width // groups, feat_width // n), f32),
            jax.ShapeDtypeStruct((1, examples), f32),
        ),
        in_specs=[hbm] * 5 + [vmem],
        out_specs=(vmem, vmem, vmem),
        scratch_shapes=[
            pltpu.VMEM((steps, 2, 2, rows // 2, depth), bf16),
            pltpu.VMEM((2, rows, depth), bf16),
            pltpu.VMEM((width, depth), bf16),
            pltpu.VMEM((tokens, width), bf16),
            pltpu.VMEM((PROJ, width), bf16),
            pltpu.VMEM((PROJ, depth), bf16),
            pltpu.VMEM((n, PROJ, rows), f32),
            pltpu.VMEM((n * chunks, EX_GRP, LANES), f32),
            pltpu.VMEM((n, chunks, EX_GRP, LANES), f32),
            pltpu.VMEM((groups, chunks, EX_GRP, LANES), f32),
            pltpu.VMEM((n, groups, chunks, EX_GRP, LANES), f32),
            pltpu.VMEM((examples, feat_width), f32),
            dma((5,)),
            dma((steps, 2)),
            dma((steps, 2)),
            dma((steps, 2)),
            dma((steps, 2)),
            dma,
            dma,
            dma((n - 1,)),
            dma((n - 1,)),
            dma((n - 1,)),
            dma((n - 1,)),
            dma((max(1, groups - 1),)),
            dma((max(1, groups - 1),)),
            dma((n - 1,)),
            dma((n - 1,)),
        ],
        compiler_params=pltpu.CompilerParams(
            collective_id=0, has_side_effects=True, vmem_limit_bytes=56 * 1024 * 1024
        ),
        cost_estimate=pl.CostEstimate(
            flops=2 * tokens * depth * width, bytes_accessed=2 * width * (depth + 2 * tokens),
            transcendentals=0,
        ),
    )(x, down_weight, h, proj_in.T, proj_out.T, ids)
    return out[None], gram, scores.reshape(examples)


def solution(mesh):
    in_specs = (
        P("grp", None, "fsdp"),
        P("grp", "fsdp", None),
        P("fsdp", None),
        P("fsdp", None),
        P(),
        P("grp", None),
    )
    out_specs = (P("grp", None, "fsdp"), P("grp", "fsdp"), P())
    return jax.shard_map(body, mesh=mesh, in_specs=in_specs, out_specs=out_specs, check_vma=False)
```

time: 354 us -> 121 us (0.34)
  waiting for transfers between devices: 292 us -> 0 us
  Pallas kernels: 0 us -> 114 us
  matrix products: 35.8 us -> 0 us
  between operations: 14.5 us -> 0.65 us
  other arithmetic: 5.33 us -> 0 us
  blocking collectives: 5 us -> 0 us
  local copies, waits for them, and re-layouts: 1.65 us -> 6.15 us
    pallas_call x0 -> x1, Pallas kernels: none -> 114 us  [body(): pl.pallas_call(functools.partial(kernel, n, groups, scale), out_shape=(ja...]
    all_gather x1 -> x0, waiting for transfers between devices: 114 us -> none  [body(): grad_full = lax.all_gather(grad_rows, 'fsdp', axis=0, tiled=True)]
    reduce_scatter x2 -> x0, waiting for transfers between devices: 90 us -> none  [the longest x1 58.1 us: body(): lax.psum_scatter(jnp.dot(rows_part, proj_in, preferred_element_type=jnp.f...]
    psum x1 -> x0, waiting for transfers between devices: 87.4 us -> none  [body(): group_feats = lax.psum(partial_feats, 'fsdp')]
    dot_general x6 -> x0, matrix products: 35.6 us -> none  [the longest x1 23.4 us: body(): lax.dot_general(grad_full, down_weight, (((1,), (1,)), ((), ())), preferr...]
    unnamed x6 -> x7, local copies, waits for them, and re-layouts: 0.02 us -> 6.15 us
    all_gather x1 -> x0, blocking collectives: 5 us -> none  [body(): lax.all_gather(group_feats.astype(jnp.bfloat16), 'grp', axis=0, tiled=True)]
    another operation x5 -> x0, other arithmetic: 4 us -> none  [the longest x3 2.12 us: inverse_diagonal(): lower = jnp.linalg.cholesky(matrix)]
  transfers between devices with their start and end apart: 4 -> 0, of which waited for: 4 -> 0; matrix products, arithmetic and copies ran while one was open for 10% -> 0% of each run, Pallas kernels for 0% -> 0%
where the time goes in v1:
time: 121 us
  Pallas kernels  114 us (94%)
  local copies, waits for them, and re-layouts  6.15 us (5%)
    pallas_call x1, Pallas kernels, body(): pl.pallas_call(functools.partial(kernel, n, groups, scale), out_shape=(ja...  114 us
    unnamed x7, local copies, waits for them, and re-layouts  6.15 us

profile of v1, /device:TPU:0, one launch (start us, length us, event | category | flops | bytes accessed | tf_op | source)
XLA Modules:
  0.0 120.6 jit_solution(1782994816113680999)
XLA Ops:
  0.6 113.8 %shard_map.85 = (bf16[2048,896]{1,0:T(8,128)(2,1)}, f32[2048,256]{1,0:T(8,128)}, f32[1,16]{1,0:T(1,128)}) custom-call(bf16[128,4096]{1,0:T(8,128)(2,1)} %bitcast.9, bf16[896,4096]{1,0:T(8,128)(2,1)} %w_hbm.1, bf16[2048,896]{1,0:T(8,128)(2,1)} %bitcast.8, bf16[64,896]{1,0:T(8,128)(2,1)} %bitcast.11, bf16[64,4096]{1,0:T(8,128)(2,1)} %bitcast.10, ...), custom_call_target="tpu_custom_call" | custom-call | flops 15032385536 | bytes 14680064 | tf_op jit(solution)/shard_map/pallas_call | solution.py:338
  114.4 0.0 copy-start
  114.4 4.3 %copy.12 = bf16[1,2048,896]{2,1,0:T(8,128)(2,1)} copy(bf16[1,2048,896]{2,1,0:T(8,128)(2,1)} %bitcast.7) | data formatting | bytes 7340032
  118.8 0.0 copy-done
  118.8 0.0 copy-start.1
  118.8 1.3 %copy.13 = f32[2048,256]{1,0:T(8,128)} copy(f32[2048,256]{1,0:T(8,128)S(1)} %copy-done) | data formatting | bytes 4194304
  120.1 0.0 copy-done.1
  120.1 0.5 copy.14
Async XLA Ops:
  114.4 4.3 %copy-start = (f32[2048,256]{1,0:T(8,128)S(1)}, f32[2048,256]{1,0:T(8,128)}, u32[]{:S(2)}) copy-start(f32[2048,256]{1,0:T(8,128)} %get-tuple-element.13) | copy-start | bytes 6291460
  118.8 1.3 %copy-start.1 = (f32[1,16]{1,0:T(1,128)S(1)}, f32[1,16]{1,0:T(1,128)}, u32[]{:S(2)}) copy-start(f32[1,16]{1,0:T(1,128)} %get-tuple-element.8) | copy-start | bytes 196

commit v2 on v1

--- a/solution.py
+++ b/solution.py
@@ -23,9 +23,10 @@
 def kernel(
     n, groups, scale,
     x_hbm, w_hbm, h_hbm, pin_hbm, pout_hbm, ids_ref,
-    out_ref, gram_ref, score_ref,
-    gath, own, w, h, pin, pout, rts, part, red, cross, feats, flat,
-    local_sem, ring_send, ring_recv, sib_send, sib_recv, own_send, own_recv,
+    out_hbm, gram_hbm, score_ref,
+    gath, own, w, h, pin, pout, rts, part, other, red, feats, flat, out, gram,
+    local_sem, out_sem, gram_sem, ring_send, ring_recv, sib_send, sib_recv,
+    relay_send, relay_recv,
     rt_send, rt_recv, red_send, red_recv, x_send, x_recv, f_send, f_recv,
 ):
     chips = n // 2
@@ -34,9 +35,9 @@
     rows = x_hbm.shape[0]
     half = rows // 2
     width = w_hbm.shape[0]
-    chunks = part.shape[0] // n
+    chunks = part.shape[2]
     examples = groups * EX_GRP
-    gram_rows = gram_ref.shape[0]
+    gram_rows = gram.shape[0]
 
     me = lax.axis_index("fsdp")
     grp = lax.axis_index("grp")
@@ -55,11 +56,11 @@
     left = chip_at(pos - 1) * 2 + core
     sibling = chip * 2 + (1 - core)
 
+    def chip_on(p):
+        return lax.rem(chip + p, chips)
+
     def peer(p):
-        return lax.rem(me + p, n)
-
-    def source(p):
-        return lax.rem(me + n - p, n)
+        return chip_on(p) * 2 + core
 
     def remote(src, dst, send, recv, **where):
         return pltpu.make_async_remote_copy(
@@ -82,12 +83,13 @@
         pl.semaphore_signal(barrier, inc=1, device_id={"fsdp": peer(p)}, device_id_type=MESH)
         return carry
 
-    lax.fori_loop(1, n, greet, 0)
+    lax.fori_loop(1, chips, greet, 0)
+    pl.semaphore_signal(barrier, inc=1, device_id={"fsdp": sibling}, device_id_type=MESH)
     for k in range(1, groups):
         pl.semaphore_signal(
             barrier, inc=1, device_id={"grp": lax.rem(grp + k, groups)}, device_id_type=MESH
         )
-    pl.semaphore_wait(barrier, n - 1 + groups - 1)
+    pl.semaphore_wait(barrier, chips + groups - 1)
 
     def first(s, way):
         part_of = s % 2 if way == 0 else 1 - s % 2
@@ -111,27 +113,33 @@
     for s in range(min(2, steps)):
         for way in range(2):
             first(s, way).start()
-    own_copy = remote(x_hbm, own.at[1], own_send, own_recv, fsdp=sibling)
+    def relay(i, src, dst):
+        return remote(src, dst, relay_send.at[i], relay_recv.at[i], fsdp=sibling)
+
+    own_copy = relay(0, x_hbm, own.at[1])
+    rt_relay = relay(1, rts.at[core], rts.at[core])
+    part_relay = relay(2, part.at[1 - core], other)
+    feats_relay = relay(3, feats.at[grp, core], feats.at[grp, core])
     own_copy.start()
 
     def rt_copy(p):
-        return remote(rts.at[me], rts.at[me], rt_send.at[p - 1], rt_recv.at[p - 1], fsdp=peer(p))
+        mine = rts.at[core, chip]
+        return remote(mine, mine, rt_send.at[p - 1], rt_recv.at[p - 1], fsdp=peer(p))
 
     def red_copy(p):
         return remote(
-            part.at[pl.ds(peer(p) * chunks, chunks)], red.at[me],
+            part.at[core, chip_on(p)], red.at[chip],
             red_send.at[p - 1], red_recv.at[p - 1], fsdp=peer(p),
         )
+
+    def f_copy(p):
+        mine = feats.at[grp, core, chip]
+        return remote(mine, mine, f_send.at[p - 1], f_recv.at[p - 1], fsdp=peer(p))
 
     def x_copy(k):
         return remote(
-            cross.at[grp], cross.at[grp], x_send.at[k - 1], x_recv.at[k - 1],
+            feats.at[grp], feats.at[grp], x_send.at[k - 1], x_recv.at[k - 1],
             grp=lax.rem(grp + k, groups),
-        )
-
-    def f_copy(p):
-        return remote(
-            feats.at[me], feats.at[me], f_send.at[p - 1], f_recv.at[p - 1], fsdp=peer(p)
         )
 
     def over_peers(action):
@@ -139,36 +147,48 @@
             action(p)
             return carry
 
-        lax.fori_loop(1, n, step, 0)
+        lax.fori_loop(1, chips, step, 0)
 
     loads[0].wait()
     loads[1].wait()
-    rts[me] = dot(pout[...], own[0], NT)
+    rts[core, chip] = dot(pout[...], own[0], NT)
     over_peers(lambda p: rt_copy(p).start())
 
-    def multiply(block, places):
-        count = len(places)
-        size = block.shape[0] // count
+    def out_copies(unit, places):
+        return [
+            pltpu.make_async_copy(
+                out.at[unit, pl.ds(i * half, half)],
+                out_hbm.at[pl.ds(pl.multiple_of(place, half), half)],
+                out_sem.at[unit, i],
+            )
+            for i, place in enumerate(places)
+        ]
+
+    def multiply(unit, block, places):
         for start in range(0, width, 256):
             stop = min(width, start + 256)
-            product = dot(block, w[start:stop, :], NT).astype(out_ref.dtype)
-            for i, place in enumerate(places):
-                out_ref[pl.ds(pl.multiple_of(place, size), size), start:stop] = product[
-                    i * size:(i + 1) * size
-                ]
+            out[unit, :, start:stop] = dot(block, w[start:stop, :], NT).astype(out.dtype)
+        for copy in out_copies(unit, places):
+            copy.start()
 
     loads[4].wait()
     own_copy.wait_recv()
-    multiply(own[...].reshape(2 * rows, -1), (me * rows, sibling * rows))
+    own_places = (me * rows, me * rows + half, sibling * rows, sibling * rows + half)
+    multiply(0, own[...].reshape(2 * rows, -1), own_places)
+    over_peers(lambda p: rt_copy(p).wait_recv())
+    rt_relay.start()
 
     def partial_feats():
         loads[2].wait()
         loads[3].wait()
-        over_peers(lambda p: rt_copy(p).wait_recv())
+        rt_relay.wait_recv()
         r = lax.broadcasted_iota(jnp.int32, (PROJ, PROJ), 0)
         c = lax.broadcasted_iota(jnp.int32, (PROJ, PROJ), 1)
         mid = PROJ // 2
-        wanted = jnp.where(r < mid, 2 * r, 2 * (r - mid) + 1)
+        odd = lax.div(r, mid)
+        spot = lax.rem(r, mid)
+        holder = 2 * lax.div(lax.rem(spot, mid // 2), chunks) + lax.div(spot, mid // 2)
+        wanted = 2 * (holder * chunks + lax.rem(spot, chunks)) + odd
         order = jnp.where(c == wanted, 1.0, 0.0).astype(jnp.bfloat16)
         sorted_in = lax.dot_general(
             order, pin[...], (((1,), (0,)), ((), ())), preferred_element_type=jnp.float32
@@ -181,7 +201,7 @@
             piece = h[pl.ds(pl.multiple_of(b * rows, rows), rows), :]
             left_t = dot(sorted_in, piece, NT)
             onehot = jnp.where(ids_ref[b] == which, 1.0, 0.0)
-            right_t = rts[b]
+            right_t = rts[lax.rem(b, 2), lax.div(b, 2)]
             total = part[...].reshape(mid * EX_GRP, LANES)
             for i, pair in enumerate(((right_t, blank), (blank, right_t))):
                 rows_of = left_t[i * mid:(i + 1) * mid]
@@ -191,43 +211,54 @@
             return carry
 
         lax.fori_loop(0, n, block, 0)
+        part_relay.start()
+
+    def reduce_chip():
+        part_relay.wait_recv()
+        part[core] = part[core] + other[...]
         over_peers(lambda p: red_copy(p).start())
 
     def reduce_feats():
         over_peers(lambda p: red_copy(p).wait_recv())
-        total = part[pl.ds(me * chunks, chunks)]
 
         def add(p, total):
-            return total + red[source(p)]
-
-        cross[grp] = lax.fori_loop(1, n, add, total) * scale
+            return total + red[lax.rem(chip + chips - p, chips)]
+
+        feats[grp, core, chip] = lax.fori_loop(1, chips, add, part[core, chip]) * scale
+        over_peers(lambda p: f_copy(p).start())
+
+    def share_chip():
+        over_peers(lambda p: f_copy(p).wait_recv())
+        feats_relay.start()
+
+    def share_groups():
+        feats_relay.wait_recv()
         for k in range(1, groups):
             x_copy(k).start()
 
-    def share_feats():
+    gram_copy = pltpu.make_async_copy(gram, gram_hbm, gram_sem)
+
+    def gram_block():
         for k in range(1, groups):
             x_copy(k).wait_recv()
-        feats[me] = cross[...]
-        over_peers(lambda p: f_copy(p).start())
-
-    def gram_block():
-        over_peers(lambda p: f_copy(p).wait_recv())
         for q in range(n):
             for m in range(chunks):
                 column = (q * chunks + m) * LANES
-                flat[:, column:column + LANES] = feats[q, :, m].reshape(examples, LANES)
+                piece = feats[:, q % 2, q // 2, m].reshape(examples, LANES)
+                flat[:, column:column + LANES] = piece
         cols = chunks * LANES
         mine = flat[:, pl.ds(pl.multiple_of(me * cols, cols), cols)] * (1.0 / examples)
         tile = min(512, gram_rows)
 
         def rows_of(t, carry):
             at = pl.multiple_of(grp * gram_rows + t * tile, tile)
-            gram_ref[pl.ds(pl.multiple_of(t * tile, tile), tile), :] = dot(
+            gram[pl.ds(pl.multiple_of(t * tile, tile), tile), :] = dot(
                 flat[:, pl.ds(at, tile)], mine, TN, HIGH
             )
             return carry
 
         lax.fori_loop(0, gram_rows // tile, rows_of, 0)
+        gram_copy.start()
 
     def score():
         every = flat[...]
@@ -251,7 +282,18 @@
         diagonal = jnp.sum(jnp.where(r == c, inverse, 0.0), axis=0, keepdims=True)
         score_ref[...] = 1.0 - ridge * diagonal
 
-    phases = (partial_feats, reduce_feats, share_feats, gram_block, score)
+    phases = (
+        (0, True, partial_feats), (1, True, reduce_chip), (1, False, reduce_feats),
+        (2, False, share_chip), (3, True, share_groups), (4, True, gram_block), (5, True, score),
+    )
+
+    def run_phases(s, early):
+        for at, when, phase in phases:
+            if steps > 5:
+                if when == early:
+                    pl.when(s == at)(phase)
+            elif early:
+                pl.when(s == min(at, steps - 1))(phase)
 
     def places(s):
         distance = lax.div(s, 2) + 1
@@ -267,7 +309,7 @@
     def finish(s):
         for way in range(2):
             across(s, way).wait_recv()
-        multiply(gath[s].reshape(4 * half, -1), places(s))
+        multiply(s + 1, gath[s].reshape(4 * half, -1), places(s))
 
     def ring(s, carry):
         for way in range(2):
@@ -282,13 +324,13 @@
 
             across(s, way).start()
 
-        for k, phase in enumerate(phases):
-            pl.when(s == min(k, steps - 1))(phase)
+        run_phases(s, True)
 
         @pl.when(s > 0)
         def _():
             finish(s - 1)
 
+        run_phases(s, False)
         return carry
 
     lax.fori_loop(0, steps, ring, 0)
@@ -311,11 +353,22 @@
         return carry
 
     lax.fori_loop(2, steps, sent_on, 0)
-    own_copy.wait_send()
+    for copy in (own_copy, rt_relay, part_relay, feats_relay):
+        copy.wait_send()
     for copies in (rt_copy, red_copy, f_copy):
         over_peers(lambda p: copies(p).wait_send())
     for k in range(1, groups):
         x_copy(k).wait_send()
+    gram_copy.wait()
+    for copy in out_copies(0, own_places):
+        copy.wait()
+
+    def written(s, carry):
+        for copy in out_copies(s + 1, places(s)):
+            copy.wait()
+        return carry
+
+    lax.fori_loop(0, steps, written, 0)
 
 
 def body(hidden_act, grad_output, down_weight, proj_in, proj_out, example_ids):
@@ -325,7 +378,8 @@
     x = grad_output[0]
     rows, depth = x.shape
     tokens, width = h.shape
-    steps = n // 2 - 1
+    chips = n // 2
+    steps = chips - 1
     feat_width = PROJ * PROJ
     examples = EX_GRP * groups
     chunks = feat_width // LANES // n
@@ -343,7 +397,7 @@
             jax.ShapeDtypeStruct((1, examples), f32),
         ),
         in_specs=[hbm] * 5 + [vmem],
-        out_specs=(vmem, vmem, vmem),
+        out_specs=(hbm, hbm, vmem),
         scratch_shapes=[
             pltpu.VMEM((steps, 2, 2, rows // 2, depth), bf16),
             pltpu.VMEM((2, rows, depth), bf16),
@@ -351,30 +405,34 @@
             pltpu.VMEM((tokens, width), bf16),
             pltpu.VMEM((PROJ, width), bf16),
             pltpu.VMEM((PROJ, depth), bf16),
-            pltpu.VMEM((n, PROJ, rows), f32),
-            pltpu.VMEM((n * chunks, EX_GRP, LANES), f32),
-            pltpu.VMEM((n, chunks, EX_GRP, LANES), f32),
-            pltpu.VMEM((groups, chunks, EX_GRP, LANES), f32),
-            pltpu.VMEM((n, groups, chunks, EX_GRP, LANES), f32),
+            pltpu.VMEM((2, chips, PROJ, rows), f32),
+            pltpu.VMEM((2, chips, chunks, EX_GRP, LANES), f32),
+            pltpu.VMEM((chips, chunks, EX_GRP, LANES), f32),
+            pltpu.VMEM((chips, chunks, EX_GRP, LANES), f32),
+            pltpu.VMEM((groups, 2, chips, chunks, EX_GRP, LANES), f32),
             pltpu.VMEM((examples, feat_width), f32),
+            pltpu.VMEM((steps + 1, 2 * rows, width), bf16),
+            pltpu.VMEM((feat_width // groups, feat_width // n), f32),
             dma((5,)),
+            dma((steps + 1, 4)),
+            dma,
             dma((steps, 2)),
             dma((steps, 2)),
             dma((steps, 2)),
             dma((steps, 2)),
-            dma,
-            dma,
-            dma((n - 1,)),
-            dma((n - 1,)),
-            dma((n - 1,)),
-            dma((n - 1,)),
+            dma((4,)),
+            dma((4,)),
+            dma((chips - 1,)),
+            dma((chips - 1,)),
+            dma((chips - 1,)),
+            dma((chips - 1,)),
             dma((max(1, groups - 1),)),
             dma((max(1, groups - 1),)),
-            dma((n - 1,)),
-            dma((n - 1,)),
+            dma((chips - 1,)),
+            dma((chips - 1,)),
         ],
         compiler_params=pltpu.CompilerParams(
-            collective_id=0, has_side_effects=True, vmem_limit_bytes=56 * 1024 * 1024
+            collective_id=0, has_side_effects=True, vmem_limit_bytes=44 * 1024 * 1024
         ),
         cost_estimate=pl.CostEstimate(
             flops=2 * tokens * depth * width, bytes_accessed=2 * width * (depth + 2 * tokens),

time: 121 us -> 116 us (0.959)
  Pallas kernels: 114 us -> 107 us
  local copies, waits for them, and re-layouts: 6.15 us -> 7.52 us
    pallas_call x1, Pallas kernels: 114 us -> 107 us  [body(): pl.pallas_call(functools.partial(kernel, n, groups, scale), out_shape=(ja...]
    unnamed x7 -> x11, local copies, waits for them, and re-layouts: 6.15 us -> 7.52 us
where the time goes in v2:
time: 116 us; the launch traced here: 115 us
  Pallas kernels  107 us (92%)
  local copies, waits for them, and re-layouts  7.52 us (6%)
    pallas_call x1, Pallas kernels, body(): pl.pallas_call(functools.partial(kernel, n, groups, scale), out_shape=(ja...  107 us
    unnamed x11, local copies, waits for them, and re-layouts  7.52 us

profile of v2, /device:TPU:0, one launch (start us, length us, event | category | flops | bytes accessed | tf_op | source)
XLA Modules:
  0.0 115.4 jit_solution(16838695002398801065)
XLA Ops:
  0.6 0.0 copy-start
  0.6 1.2 %copy-done = bf16[1,128,4096]{2,1,0:T(8,128)(2,1)S(1)} copy-done((bf16[1,128,4096]{2,1,0:T(8,128)(2,1)S(1)}, bf16[1,128,4096]{2,1,0:T(8,128)(2,1)}, u32[]{:S(2)}) %copy-start) | copy-done | bytes 1048600
  1.9 0.0 copy-start.1
  1.9 1.0 copy-done.1
  2.9 0.0 copy-start.2
  2.9 0.9 copy-done.2
  3.8 0.0 copy-start.3
  3.8 0.7 copy-done.3
  4.5 107.2 %shard_map.85 = (bf16[2048,896]{1,0:T(8,128)(2,1)S(1)}, f32[2048,256]{1,0:T(8,128)S(1)}, f32[1,16]{1,0:T(1,128)S(1)}) custom-call(bf16[128,4096]{1,0:T(8,128)(2,1)S(1)} %bitcast.8, bf16[896,4096]{1,0:T(8,128)(2,1)} %w_hbm.1, bf16[2048,896]{1,0:T(8,128)(2,1)} %bitcast.13, bf16[64,896]{1,0:T(8,128)(2,1)S(1)} %bitcast.10, bf16[64,4096]{1,0:T(8,128)(2,1)S(1)} %bitcast.9, ...), custom_call_target="tpu_custom_call" | custom-call | flops 15032385536 | bytes 14680064 | tf_op jit(solution)/shard_map/pallas_call | solution.py:392
  111.7 1.8 %copy.12 = bf16[1,2048,896]{2,1,0:T(8,128)(2,1)} copy(bf16[1,2048,896]{2,1,0:T(8,128)(2,1)S(1)} %bitcast.7) | data formatting | bytes 7340032
  113.5 1.3 %copy.13 = f32[2048,256]{1,0:T(8,128)} copy(f32[2048,256]{1,0:T(8,128)S(1)} %get-tuple-element.13) | data formatting | bytes 4194304
  114.8 0.5 copy.14
Async XLA Ops:
  0.6 1.2 %copy-start = (bf16[1,128,4096]{2,1,0:T(8,128)(2,1)S(1)}, bf16[1,128,4096]{2,1,0:T(8,128)(2,1)}, u32[]{:S(2)}) copy-start(bf16[1,128,4096]{2,1,0:T(8,128)(2,1)} %param.7) | copy-start | bytes 3145732
  1.9 1.0 copy-start.1
  2.9 0.9 copy-start.2
  3.8 0.7 copy-start.3

commit v3 on v2

--- a/solution.py
+++ b/solution.py
@@ -22,11 +22,11 @@
 
 def kernel(
     n, groups, scale,
-    x_hbm, w_hbm, h_hbm, pin_hbm, pout_hbm, ids_ref,
+    x_hbm, w_hbm, h_hbm, pin_hbm, pout_hbm, ids_hbm,
     out_hbm, gram_hbm, score_ref,
-    gath, own, w, h, pin, pout, rts, part, other, red, feats, flat, out, gram,
+    gath, own, w, h, pin, pout, ids, rts, part, other, red, feats, flat, out, gram,
     local_sem, out_sem, gram_sem, ring_send, ring_recv, sib_send, sib_recv,
-    relay_send, relay_recv,
+    relay_send, relay_recv, flip_send, flip_recv,
     rt_send, rt_recv, red_send, red_recv, x_send, x_recv, f_send, f_recv,
 ):
     chips = n // 2
@@ -71,7 +71,7 @@
     loads = [
         pltpu.make_async_copy(src, dst, local_sem.at[i])
         for i, (src, dst) in enumerate(
-            ((x_hbm, own.at[0]), (pout_hbm, pout), (h_hbm, h), (pin_hbm, pin), (w_hbm, w))
+            ((x_hbm, own.at[0]), (pout_hbm, pout), (w_hbm, w), (pin_hbm, pin), (ids_hbm, ids), (h_hbm, h))
         )
     ]
     for load in loads:
@@ -89,6 +89,9 @@
         pl.semaphore_signal(
             barrier, inc=1, device_id={"grp": lax.rem(grp + k, groups)}, device_id_type=MESH
         )
+    loads[0].wait()
+    loads[1].wait()
+    rts[core, side, along] = dot(pout[...], own[0], NT)
     pl.semaphore_wait(barrier, chips + groups - 1)
 
     def first(s, way):
@@ -110,6 +113,20 @@
             sib_send.at[s, way], sib_recv.at[s, way], fsdp=sibling,
         )
 
+    def rt_copy(p):
+        mine = rts.at[core, side, along]
+        return remote(mine, mine, rt_send.at[p - 1], rt_recv.at[p - 1], fsdp=peer(2 * p))
+
+    def over_line(action):
+        def step(p, carry):
+            action(p)
+            return carry
+
+        lax.fori_loop(1, half_chips, step, 0)
+
+    flip = (2 * along + 1 - side) * 2 + core
+    rt_flip = remote(rts.at[core, side], rts.at[core, side], flip_send, flip_recv, fsdp=flip)
+    over_line(lambda p: rt_copy(p).start())
     for s in range(min(2, steps)):
         for way in range(2):
             first(s, way).start()
@@ -122,10 +139,6 @@
     feats_relay = relay(3, feats.at[grp, core], feats.at[grp, core])
     own_copy.start()
 
-    def rt_copy(p):
-        mine = rts.at[core, chip]
-        return remote(mine, mine, rt_send.at[p - 1], rt_recv.at[p - 1], fsdp=peer(p))
-
     def red_copy(p):
         return remote(
             part.at[core, chip_on(p)], red.at[chip],
@@ -148,11 +161,6 @@
             return carry
 
         lax.fori_loop(1, chips, step, 0)
-
-    loads[0].wait()
-    loads[1].wait()
-    rts[core, chip] = dot(pout[...], own[0], NT)
-    over_peers(lambda p: rt_copy(p).start())
 
     def out_copies(unit, places):
         return [
@@ -171,16 +179,20 @@
         for copy in out_copies(unit, places):
             copy.start()
 
-    loads[4].wait()
+    loads[2].wait()
     own_copy.wait_recv()
     own_places = (me * rows, me * rows + half, sibling * rows, sibling * rows + half)
     multiply(0, own[...].reshape(2 * rows, -1), own_places)
-    over_peers(lambda p: rt_copy(p).wait_recv())
-    rt_relay.start()
+    over_line(lambda p: rt_copy(p).wait_recv())
+    rt_flip.start()
+
+    def share_right():
+        rt_flip.wait_recv()
+        rt_relay.start()
 
     def partial_feats():
-        loads[2].wait()
-        loads[3].wait()
+        for load in loads[3:]:
+            load.wait()
         rt_relay.wait_recv()
         r = lax.broadcasted_iota(jnp.int32, (PROJ, PROJ), 0)
         c = lax.broadcasted_iota(jnp.int32, (PROJ, PROJ), 1)
@@ -195,18 +207,27 @@
         ).astype(jnp.bfloat16)
         part[...] = jnp.zeros_like(part)
         which = lax.broadcasted_iota(jnp.int32, (EX_GRP, rows), 0)
-        blank = jnp.zeros((PROJ, rows), jnp.float32)
+        blank = jnp.zeros((PROJ, rows), jnp.bfloat16)
+
+        def halves(a):
+            high = a.astype(jnp.bfloat16)
+            return high, (a - high.astype(jnp.float32)).astype(jnp.bfloat16)
 
         def block(b, carry):
             piece = h[pl.ds(pl.multiple_of(b * rows, rows), rows), :]
             left_t = dot(sorted_in, piece, NT)
-            onehot = jnp.where(ids_ref[b] == which, 1.0, 0.0)
-            right_t = rts[lax.rem(b, 2), lax.div(b, 2)]
+            onehot = jnp.where(ids[b] == which, 1.0, 0.0)
+            right_high, right_low = halves(
+                rts[lax.rem(b, 2), lax.rem(lax.div(b, 2), 2), lax.div(b, 4)]
+            )
             total = part[...].reshape(mid * EX_GRP, LANES)
-            for i, pair in enumerate(((right_t, blank), (blank, right_t))):
+            for i in range(2):
                 rows_of = left_t[i * mid:(i + 1) * mid]
                 weighted = (rows_of[:, None, :] * onehot[None]).reshape(mid * EX_GRP, rows)
-                total += dot(weighted, jnp.concatenate(pair, axis=0), NT, HIGH)
+                high, low = halves(weighted)
+                for a, r in ((high, right_high), (high, right_low), (low, right_high)):
+                    pair = (blank, r) if i else (r, blank)
+                    total += dot(a, jnp.concatenate(pair, axis=0), NT)
             part[...] = total.reshape(part.shape)
             return carry
 
@@ -283,8 +304,9 @@
         score_ref[...] = 1.0 - ridge * diagonal
 
     phases = (
-        (0, True, partial_feats), (1, True, reduce_chip), (1, False, reduce_feats),
-        (2, False, share_chip), (3, True, share_groups), (4, True, gram_block), (5, True, score),
+        (0, False, share_right), (1, True, partial_feats), (1, False, reduce_chip),
+        (2, False, reduce_feats), (3, False, share_chip), (4, True, share_groups),
+        (4, False, gram_block), (5, False, score),
     )
 
     def run_phases(s, early):
@@ -325,16 +347,11 @@
             across(s, way).start()
 
         run_phases(s, True)
-
-        @pl.when(s > 0)
-        def _():
-            finish(s - 1)
-
+        finish(s)
         run_phases(s, False)
         return carry
 
     lax.fori_loop(0, steps, ring, 0)
-    finish(steps - 1)
 
     def sent(s, carry):
         for way in range(2):
@@ -353,9 +370,10 @@
         return carry
 
     lax.fori_loop(2, steps, sent_on, 0)
-    for copy in (own_copy, rt_relay, part_relay, feats_relay):
+    for copy in (own_copy, rt_flip, rt_relay, part_relay, feats_relay):
         copy.wait_send()
-    for copies in (rt_copy, red_copy, f_copy):
+    over_line(lambda p: rt_copy(p).wait_send())
+    for copies in (red_copy, f_copy):
         over_peers(lambda p: copies(p).wait_send())
     for k in range(1, groups):
         x_copy(k).wait_send()
@@ -379,6 +397,7 @@
     rows, depth = x.shape
     tokens, width = h.shape
     chips = n // 2
+    half_chips = chips // 2
     steps = chips - 1
     feat_width = PROJ * PROJ
     examples = EX_GRP * groups
@@ -389,6 +408,7 @@
     dma = pltpu.SemaphoreType.DMA
     vmem = pl.BlockSpec(memory_space=pltpu.VMEM)
     hbm = pl.BlockSpec(memory_space=pl.ANY)
+    pinned = pl.BlockSpec(memory_space=pltpu.HBM)
     out, gram, scores = pl.pallas_call(
         functools.partial(kernel, n, groups, scale),
         out_shape=(
@@ -396,7 +416,7 @@
             jax.ShapeDtypeStruct((feat_width // groups, feat_width // n), f32),
             jax.ShapeDtypeStruct((1, examples), f32),
         ),
-        in_specs=[hbm] * 5 + [vmem],
+        in_specs=[pinned] * 6,
         out_specs=(hbm, hbm, vmem),
         scratch_shapes=[
             pltpu.VMEM((steps, 2, 2, rows // 2, depth), bf16),
@@ -405,7 +425,8 @@
             pltpu.VMEM((tokens, width), bf16),
             pltpu.VMEM((PROJ, width), bf16),
             pltpu.VMEM((PROJ, depth), bf16),
-            pltpu.VMEM((2, chips, PROJ, rows), f32),
+            pltpu.VMEM((n, 1, rows), jnp.int32),
+            pltpu.VMEM((2, 2, chips // 2, PROJ, rows), f32),
             pltpu.VMEM((2, chips, chunks, EX_GRP, LANES), f32),
             pltpu.VMEM((chips, chunks, EX_GRP, LANES), f32),
             pltpu.VMEM((chips, chunks, EX_GRP, LANES), f32),
@@ -413,7 +434,7 @@
             pltpu.VMEM((examples, feat_width), f32),
             pltpu.VMEM((steps + 1, 2 * rows, width), bf16),
             pltpu.VMEM((feat_width // groups, feat_width // n), f32),
-            dma((5,)),
+            dma((6,)),
             dma((steps + 1, 4)),
             dma,
             dma((steps, 2)),
@@ -422,8 +443,10 @@
             dma((steps, 2)),
             dma((4,)),
             dma((4,)),
-            dma((chips - 1,)),
-            dma((chips - 1,)),
+            dma,
+            dma,
+            dma((half_chips - 1,)),
+            dma((half_chips - 1,)),
             dma((chips - 1,)),
             dma((chips - 1,)),
             dma((max(1, groups - 1),)),

time: 116 us -> 105 us (0.905)
  Pallas kernels: 107 us -> 95.8 us
    pallas_call x1, Pallas kernels: 107 us -> 95.8 us  [body(): pl.pallas_call(functools.partial(kernel, n, groups, scale), out_shape=(ja...]
where the time goes in v3:
time: 105 us; the launch traced here: 104 us
  Pallas kernels  95.8 us (91%)
  local copies, waits for them, and re-layouts  7.52 us (7%)
    pallas_call x1, Pallas kernels, body(): pl.pallas_call(functools.partial(kernel, n, groups, scale), out_shape=(ja...  95.8 us
    unnamed x11, local copies, waits for them, and re-layouts  7.52 us

profile of v3, /device:TPU:0, one launch (start us, length us, event | category | flops | bytes accessed | tf_op | source)
XLA Modules:
  0.0 103.9 jit_solution(6308980014017265167)
XLA Ops:
  0.6 0.0 copy-start
  0.6 1.2 %copy-done = bf16[1,128,4096]{2,1,0:T(8,128)(2,1)S(1)} copy-done((bf16[1,128,4096]{2,1,0:T(8,128)(2,1)S(1)}, bf16[1,128,4096]{2,1,0:T(8,128)(2,1)}, u32[]{:S(2)}) %copy-start) | copy-done | bytes 1048600
  1.9 0.0 copy-start.1
  1.9 1.0 copy-done.1
  2.9 0.0 copy-start.2
  2.9 0.9 copy-done.2
  3.8 0.0 copy-start.3
  3.8 0.7 copy-done.3
  4.5 95.8 %shard_map.85 = (bf16[2048,896]{1,0:T(8,128)(2,1)S(1)}, f32[2048,256]{1,0:T(8,128)S(1)}, f32[1,16]{1,0:T(1,128)S(1)}) custom-call(bf16[128,4096]{1,0:T(8,128)(2,1)S(1)} %bitcast.8, bf16[896,4096]{1,0:T(8,128)(2,1)} %w_hbm.1, bf16[2048,896]{1,0:T(8,128)(2,1)} %bitcast.13, bf16[64,896]{1,0:T(8,128)(2,1)S(1)} %bitcast.10, bf16[64,4096]{1,0:T(8,128)(2,1)S(1)} %bitcast.9, ...), custom_call_target="tpu_custom_call" | custom-call | flops 15032385536 | bytes 14680064 | tf_op jit(solution)/shard_map/pallas_call | solution.py:412
  100.3 1.8 %copy.12 = bf16[1,2048,896]{2,1,0:T(8,128)(2,1)} copy(bf16[1,2048,896]{2,1,0:T(8,128)(2,1)S(1)} %bitcast.7) | data formatting | bytes 7340032
  102.1 1.3 %copy.13 = f32[2048,256]{1,0:T(8,128)} copy(f32[2048,256]{1,0:T(8,128)S(1)} %get-tuple-element.13) | data formatting | bytes 4194304
  103.4 0.5 copy.14
Async XLA Ops:
  0.6 1.2 %copy-start = (bf16[1,128,4096]{2,1,0:T(8,128)(2,1)S(1)}, bf16[1,128,4096]{2,1,0:T(8,128)(2,1)}, u32[]{:S(2)}) copy-start(bf16[1,128,4096]{2,1,0:T(8,128)(2,1)} %param.7) | copy-start | bytes 3145732
  1.9 1.0 %copy-start.1 = (bf16[4096,64]{0,1:T(8,128)(2,1)S(1)}, bf16[4096,64]{0,1:T(8,128)(2,1)}, u32[]{:S(2)}) copy-start(bf16[4096,64]{0,1:T(8,128)(2,1)} %param.10) | copy-start | bytes 1572868
  2.9 0.9 copy-start.2
  3.8 0.7 copy-start.3

commit v4 on v3

--- a/solution.py
+++ b/solution.py
@@ -74,7 +74,7 @@
             ((x_hbm, own.at[0]), (pout_hbm, pout), (w_hbm, w), (pin_hbm, pin), (ids_hbm, ids), (h_hbm, h))
         )
     ]
-    for load in loads:
+    for load in loads[:2]:
         load.start()
 
     barrier = pltpu.get_barrier_semaphore()
@@ -91,6 +91,8 @@
         )
     loads[0].wait()
     loads[1].wait()
+    for load in loads[2:]:
+        load.start()
     rts[core, side, along] = dot(pout[...], own[0], NT)
     pl.semaphore_wait(barrier, chips + groups - 1)
 
@@ -461,7 +463,10 @@
             flops=2 * tokens * depth * width, bytes_accessed=2 * width * (depth + 2 * tokens),
             transcendentals=0,
         ),
-    )(x, down_weight, h, proj_in.T, proj_out.T, ids)
+    )(*[
+        pltpu.with_memory_space_constraint(operand, pltpu.HBM)
+        for operand in (x, down_weight, h, proj_in.T, proj_out.T, ids)
+    ])
     return out[None], gram, scores.reshape(examples)
 
 

time: 105 us -> 101 us (0.962)
  local copies, waits for them, and re-layouts: 7.52 us -> 3.67 us
    unnamed x11 -> x3, local copies, waits for them, and re-layouts: 7.52 us -> 3.67 us
where the time goes in v4:
time: 101 us; the launch traced here: 100 us
  Pallas kernels  95.8 us (95%)
  local copies, waits for them, and re-layouts  3.67 us (4%)
    pallas_call x1, Pallas kernels, body(): pl.pallas_call(functools.partial(kernel, n, groups, scale), out_shape=(ja...  95.8 us
    unnamed x3, local copies, waits for them, and re-layouts  3.67 us

profile of v4, /device:TPU:0, one launch (start us, length us, event | category | flops | bytes accessed | tf_op | source)
XLA Modules:
  0.0 100.1 jit_solution(12106047503802411431)
XLA Ops:
  0.6 95.8 %shard_map.85 = (bf16[2048,896]{1,0:T(8,128)(2,1)S(1)}, f32[2048,256]{1,0:T(8,128)S(1)}, f32[1,16]{1,0:T(1,128)S(1)}) custom-call(bf16[128,4096]{1,0:T(8,128)(2,1)} %bitcast.10, bf16[896,4096]{1,0:T(8,128)(2,1)} %w_hbm.1, bf16[2048,896]{1,0:T(8,128)(2,1)} %bitcast.9, bf16[64,896]{1,0:T(8,128)(2,1)} %bitcast.12, bf16[64,4096]{1,0:T(8,128)(2,1)} %bitcast.11, ...), custom_call_target="tpu_custom_call" | custom-call | flops 15032385536 | bytes 14680064 | tf_op jit(solution)/shard_map/pallas_call | solution.py:414
  96.4 1.8 %copy.12 = bf16[1,2048,896]{2,1,0:T(8,128)(2,1)} copy(bf16[1,2048,896]{2,1,0:T(8,128)(2,1)S(1)} %bitcast.7) | data formatting | bytes 7340032
  98.3 1.3 %copy.13 = f32[2048,256]{1,0:T(8,128)} copy(f32[2048,256]{1,0:T(8,128)S(1)} %get-tuple-element.13) | data formatting | bytes 4194304
  99.6 0.5 copy.14

commit v5 on v4

--- a/solution.py
+++ b/solution.py
@@ -13,6 +13,7 @@
 MESH = pl.DeviceIdType.MESH
 HIGH = lax.Precision.HIGHEST
 NT = (((1,), (1,)), ((), ()))
+NN = (((1,), (0,)), ((), ()))
 TN = (((0,), (0,)), ((), ()))
 
 
@@ -24,7 +25,7 @@
     n, groups, scale,
     x_hbm, w_hbm, h_hbm, pin_hbm, pout_hbm, ids_hbm,
     out_hbm, gram_hbm, score_ref,
-    gath, own, w, h, pin, pout, ids, rts, part, other, red, feats, flat, out, gram,
+    gath, own, w, h, pin, pout, ids, wt, rts, part, other, red, feats, flat, out, gram,
     local_sem, out_sem, gram_sem, ring_send, ring_recv, sib_send, sib_recv,
     relay_send, relay_recv, flip_send, flip_recv,
     rt_send, rt_recv, red_send, red_recv, x_send, x_recv, f_send, f_recv,
@@ -177,11 +178,19 @@
     def multiply(unit, block, places):
         for start in range(0, width, 256):
             stop = min(width, start + 256)
-            out[unit, :, start:stop] = dot(block, w[start:stop, :], NT).astype(out.dtype)
+            out[unit, :, start:stop] = dot(block, wt[:, start:stop], NN).astype(out.dtype)
         for copy in out_copies(unit, places):
             copy.start()
 
     loads[2].wait()
+    turned = min(512, w.shape[1])
+
+    def turn(t, carry):
+        at = pl.multiple_of(t * turned, turned)
+        wt[pl.ds(at, turned), :] = w[:, pl.ds(at, turned)].T
+        return carry
+
+    lax.fori_loop(0, w.shape[1] // turned, turn, 0)
     own_copy.wait_recv()
     own_places = (me * rows, me * rows + half, sibling * rows, sibling * rows + half)
     multiply(0, own[...].reshape(2 * rows, -1), own_places)
@@ -428,6 +437,7 @@
             pltpu.VMEM((PROJ, width), bf16),
             pltpu.VMEM((PROJ, depth), bf16),
             pltpu.VMEM((n, 1, rows), jnp.int32),
+            pltpu.VMEM((depth, width), bf16),
             pltpu.VMEM((2, 2, chips // 2, PROJ, rows), f32),
             pltpu.VMEM((2, chips, chunks, EX_GRP, LANES), f32),
             pltpu.VMEM((chips, chunks, EX_GRP, LANES), f32),
@@ -457,7 +467,7 @@
             dma((chips - 1,)),
         ],
         compiler_params=pltpu.CompilerParams(
-            collective_id=0, has_side_effects=True, vmem_limit_bytes=44 * 1024 * 1024
+            collective_id=0, has_side_effects=True, vmem_limit_bytes=48 * 1024 * 1024
         ),
         cost_estimate=pl.CostEstimate(
             flops=2 * tokens * depth * width, bytes_accessed=2 * width * (depth + 2 * tokens),

time: 101 us -> 101 us (level)
  no operation moved by 1% of the time
where the time goes in v5:
time: 101 us; the launch traced here: 100 us
  Pallas kernels  95.8 us (95%)
  local copies, waits for them, and re-layouts  3.67 us (4%)
    pallas_call x1, Pallas kernels, body(): pl.pallas_call(functools.partial(kernel, n, groups, scale), out_shape=(ja...  95.8 us
    unnamed x3, local copies, waits for them, and re-layouts  3.67 us

profile of v5, /device:TPU:0, one launch (start us, length us, event | category | flops | bytes accessed | tf_op | source)
XLA Modules:
  0.0 100.1 jit_solution(11614622838022056623)
XLA Ops:
  0.6 95.8 %shard_map.85 = (bf16[2048,896]{1,0:T(8,128)(2,1)S(1)}, f32[2048,256]{1,0:T(8,128)S(1)}, f32[1,16]{1,0:T(1,128)S(1)}) custom-call(bf16[128,4096]{1,0:T(8,128)(2,1)} %bitcast.10, bf16[896,4096]{1,0:T(8,128)(2,1)} %w_hbm.1, bf16[2048,896]{1,0:T(8,128)(2,1)} %bitcast.9, bf16[64,896]{1,0:T(8,128)(2,1)} %bitcast.12, bf16[64,4096]{1,0:T(8,128)(2,1)} %bitcast.11, ...), custom_call_target="tpu_custom_call" | custom-call | flops 15032385536 | bytes 14680064 | tf_op jit(solution)/shard_map/pallas_call | solution.py:423
  96.4 1.8 %copy.12 = bf16[1,2048,896]{2,1,0:T(8,128)(2,1)} copy(bf16[1,2048,896]{2,1,0:T(8,128)(2,1)S(1)} %bitcast.7) | data formatting | bytes 7340032
  98.2 1.3 %copy.13 = f32[2048,256]{1,0:T(8,128)} copy(f32[2048,256]{1,0:T(8,128)S(1)} %get-tuple-element.13) | data formatting | bytes 4194304
  99.6 0.5 copy.14

commit v6 on v4

--- a/solution.py
+++ b/solution.py
@@ -99,19 +99,19 @@
     def first(s, way):
         part_of = s % 2 if way == 0 else 1 - s % 2
         return remote(
-            x_hbm.at[pl.ds(part_of * half, half)], gath.at[s, way, 0],
+            x_hbm.at[pl.ds(part_of * half, half)], gath.at[s, 0, way],
             ring_send.at[s, way], ring_recv.at[s, way], fsdp=right if way == 0 else left,
         )
 
     def onward(s, way):
         return remote(
-            gath.at[s - 2, way, 0], gath.at[s, way, 0],
+            gath.at[s - 2, 0, way], gath.at[s, 0, way],
             ring_send.at[s, way], ring_recv.at[s, way], fsdp=right if way == 0 else left,
         )
 
     def across(s, way):
         return remote(
-            gath.at[s, way, 0], gath.at[s, way, 1],
+            gath.at[s, 0, way], gath.at[s, 1, way],
             sib_send.at[s, way], sib_recv.at[s, way], fsdp=sibling,
         )
 
@@ -174,17 +174,18 @@
             for i, place in enumerate(places)
         ]
 
-    def multiply(unit, block, places):
+    def multiply(unit, of, block, places):
         for start in range(0, width, 256):
             stop = min(width, start + 256)
-            out[unit, :, start:stop] = dot(block, w[start:stop, :], NT).astype(out.dtype)
-        for copy in out_copies(unit, places):
+            out[unit, of * rows:(of + 1) * rows, start:stop] = dot(block, w[start:stop, :], NT).astype(out.dtype)
+        for copy in out_copies(unit, places)[2 * of:2 * of + 2]:
             copy.start()
 
     loads[2].wait()
+    own_places = (me * rows, me * rows + half, sibling * rows, sibling * rows + half)
+    multiply(0, 0, own[0], own_places)
     own_copy.wait_recv()
-    own_places = (me * rows, me * rows + half, sibling * rows, sibling * rows + half)
-    multiply(0, own[...].reshape(2 * rows, -1), own_places)
+    multiply(0, 1, own[1], own_places)
     over_line(lambda p: rt_copy(p).wait_recv())
     rt_flip.start()
 
@@ -323,22 +324,23 @@
         distance = lax.div(s, 2) + 1
         which = lax.rem(s, 2)
         found = []
-        for way in range(2):
-            at = chip_at(pos - distance if way == 0 else pos + distance)
-            offset = (which if way == 0 else 1 - which) * half
-            found.append((at * 2 + core) * rows + offset)
-            found.append((at * 2 + 1 - core) * rows + offset)
+        for of in (core, 1 - core):
+            for way in range(2):
+                at = chip_at(pos - distance if way == 0 else pos + distance)
+                offset = (which if way == 0 else 1 - which) * half
+                found.append((at * 2 + of) * rows + offset)
         return found
 
     def finish(s):
+        multiply(s + 1, 0, gath[s, 0].reshape(rows, -1), places(s))
         for way in range(2):
             across(s, way).wait_recv()
-        multiply(s + 1, gath[s].reshape(4 * half, -1), places(s))
+        multiply(s + 1, 1, gath[s, 1].reshape(rows, -1), places(s))
 
     def ring(s, carry):
         for way in range(2):
             remote(
-                gath.at[s, way, 0], gath.at[s, way, 0],
+                gath.at[s, 0, way], gath.at[s, 0, way],
                 ring_send.at[s, way], ring_recv.at[s, way], fsdp=right if way == 0 else left,
             ).wait_recv()
 

time: 101 us -> 102 us (level)
  Pallas kernels: 95.8 us -> 97.5 us
    pallas_call x1, Pallas kernels: 95.8 us -> 97.5 us  [body(): pl.pallas_call(functools.partial(kernel, n, groups, scale), out_shape=(ja...]
where the time goes in v6:
time: 102 us
  Pallas kernels  97.5 us (96%)
  local copies, waits for them, and re-layouts  3.67 us (4%)
    pallas_call x1, Pallas kernels, body(): pl.pallas_call(functools.partial(kernel, n, groups, scale), out_shape=(ja...  97.5 us
    unnamed x3, local copies, waits for them, and re-layouts  3.67 us

profile of v6, /device:TPU:0, one launch (start us, length us, event | category | flops | bytes accessed | tf_op | source)
XLA Modules:
  0.0 101.9 jit_solution(7824812142668065282)
XLA Ops:
  0.6 97.5 %shard_map.85 = (bf16[2048,896]{1,0:T(8,128)(2,1)S(1)}, f32[2048,256]{1,0:T(8,128)S(1)}, f32[1,16]{1,0:T(1,128)S(1)}) custom-call(bf16[128,4096]{1,0:T(8,128)(2,1)} %bitcast.10, bf16[896,4096]{1,0:T(8,128)(2,1)} %w_hbm.1, bf16[2048,896]{1,0:T(8,128)(2,1)} %bitcast.9, bf16[64,896]{1,0:T(8,128)(2,1)} %bitcast.12, bf16[64,4096]{1,0:T(8,128)(2,1)} %bitcast.11, ...), custom_call_target="tpu_custom_call" | custom-call | flops 15032385536 | bytes 14680064 | tf_op jit(solution)/shard_map/pallas_call | solution.py:416
  98.2 1.8 %copy.12 = bf16[1,2048,896]{2,1,0:T(8,128)(2,1)} copy(bf16[1,2048,896]{2,1,0:T(8,128)(2,1)S(1)} %bitcast.7) | data formatting | bytes 7340032
  100.0 1.3 %copy.13 = f32[2048,256]{1,0:T(8,128)} copy(f32[2048,256]{1,0:T(8,128)S(1)} %get-tuple-element.13) | data formatting | bytes 4194304
  101.3 0.5 copy.14
